TPU v7x, 128 devices: a whole 4x4x4 slice. The times are simulated.
128 devices in a mesh: celly: 16 (over x, y), cellx: 8 (over z, core).
Axes of the slice: x: 4, y: 4, z: 4, core: 2. Of those that a mesh axis runs over, the one named last changes fastest.
Arguments:
- flux_blocks: bfloat16 [16384, 128, 128], P(('celly', 'cellx')), may hold values from -6 to 6
- ivar_blocks: bfloat16 [16384, 128, 128], P(('celly', 'cellx')), may hold values from 0.25 to 4
- dest_cell: int32 [16384, 1], P(('celly', 'cellx')), may hold values from 0 to 127; in each aligned block of 128 rows (0 to 127, 128 to 255, ...) at most 2 rows name the same one
- visit_id: int32 [16384], P(('celly', 'cellx')), may hold values from 0 to 19
- slot_id: int32 [16384], P(('celly', 'cellx')), may hold values from 0 to 3
- row_taps: bfloat16 [7, 41], replicated, may hold values from -1 to 1
- col_taps: bfloat16 [7, 41], replicated, may hold values from -1 to 1
- kernel_coef: float32 [20, 7, 3], replicated, may hold values from -3 to 3
Outputs:
- coadd: float32 [4096, 2048], P('celly', 'cellx')
- coadd_weight: float32 [4096, 2048], P('celly', 'cellx')
Inputs may be any that keep to these rules, and one draw needn't show every extreme that they name: `dest_cell`: no more than 2 of the 128 blocks of one device name the same cell, a bound that some block reaches.
All inputs are finite; a program needn't handle non-finite values.
Results may differ from a plain program's by a relative error of at most 0.0048.
Values may be sent and summed in bfloat16 or wider, within the bound.
A program may use at most 128 MiB of HBM per device.

v0:
```python
import jax
import jax.numpy as jnp
from jax import lax
from jax.sharding import PartitionSpec as P


def padded_2(block, sides, width):
    for axis, dim in sides:
        count = lax.axis_size(axis)
        forward = [(i, i + 1) for i in range(count - 1)]
        backward = [(target, source) for source, target in forward]
        low = lax.ppermute(
            lax.slice_in_dim(block, block.shape[dim] - width, None, axis=dim), axis, forward
        )
        high = lax.ppermute(lax.slice_in_dim(block, 0, width, axis=dim), axis, backward)
        block = jnp.concatenate([low, block, high], axis=dim)
    return block


def toeplitz_tables(taps, count, span):
    rows_index = jnp.arange(count)[:, None, None]
    cols_index = jnp.arange(span)[None, :, None]
    taps_index = jnp.arange(taps.shape[1])[None, None, :]
    picker = (cols_index - rows_index == taps_index).astype(jnp.float32)
    return jnp.einsum("ijp,bp->bij", picker, taps.astype(jnp.float32)).astype(jnp.bfloat16)


def local(flux_blocks, ivar_blocks, dest_cell, visit_id, slot_id, row_taps, col_taps, kernel_coef):
    cells_y = lax.axis_size("celly")
    cells_x = lax.axis_size("cellx")
    devices_all = cells_y * cells_x
    local_count = flux_blocks.shape[0]
    block_side = flux_blocks.shape[1]
    cell_side = 2 * block_side
    visits = kernel_coef.shape[0]
    half_rim = (row_taps.shape[1] - 1) // 2
    span = cell_side + 2 * half_rim
    capacity = max(2, (2 * local_count + devices_all - 1) // devices_all)
    slots_all = devices_all * capacity
    target_cell = dest_cell[:, 0]
    position = jnp.arange(local_count)
    earlier = (target_cell[:, None] == target_cell[None, :]) & (
        position[None, :] < position[:, None]
    )
    block_rank = jnp.sum(earlier.astype(jnp.int32), axis=1)
    target = target_cell * capacity + block_rank
    send_flux = (
        jnp.zeros((slots_all, block_side, block_side), jnp.bfloat16).at[target].set(flux_blocks)
    )
    send_ivar = (
        jnp.zeros((slots_all, block_side, block_side), jnp.bfloat16).at[target].set(ivar_blocks)
    )
    send_tags = jnp.full((slots_all,), -1, jnp.int32).at[target].set(visit_id * 4 + slot_id)
    recv_flux, recv_ivar, recv_tags = (
        lax.all_to_all(send_flux, ("celly", "cellx"), split_axis=0, concat_axis=0, tiled=True),
        lax.all_to_all(send_ivar, ("celly", "cellx"), split_axis=0, concat_axis=0, tiled=True),
        lax.all_to_all(send_tags, ("celly", "cellx"), split_axis=0, concat_axis=0, tiled=True),
    )
    keys = jnp.arange(visits * 4, dtype=jnp.int32)
    picker = (recv_tags[None, :] == keys[:, None]).astype(jnp.bfloat16)

    def place(received):
        summed = jnp.dot(
            picker,
            received.reshape(slots_all, block_side * block_side),
            preferred_element_type=jnp.float32,
        )
        summed = summed.astype(jnp.bfloat16).reshape(visits, 2, 2, block_side, block_side)
        return jnp.transpose(summed, (0, 1, 3, 2, 4)).reshape(visits, cell_side, cell_side)

    flux_planes = place(recv_flux)
    ivar_planes = place(recv_ivar)
    padded = padded_2(flux_planes, (("celly", 1), ("cellx", 2)), half_rim)
    row_table = toeplitz_tables(row_taps, cell_side, span)
    col_table = toeplitz_tables(col_taps, cell_side, span)
    top = lax.axis_index("celly") * cell_side
    left = lax.axis_index("cellx") * cell_side
    rows_pos = ((top + jnp.arange(cell_side)).astype(jnp.float32) + 0.5) * (
        2.0 / (cell_side * cells_y)
    ) - 1.0
    cols_pos = ((left + jnp.arange(cell_side)).astype(jnp.float32) + 0.5) * (
        2.0 / (cell_side * cells_x)
    ) - 1.0

    def add_visit(carry, items):
        numer, total = carry
        window, weights, coef = items
        first = jnp.einsum(
            "bip,pq->biq", row_table, window, preferred_element_type=jnp.float32
        ).astype(jnp.bfloat16)
        second = jnp.einsum("biq,bkq->bik", first, col_table, preferred_element_type=jnp.float32)
        basis_weight = (
            coef[:, 0, None, None]
            + coef[:, 1, None, None] * rows_pos[None, :, None]
            + coef[:, 2, None, None] * cols_pos[None, None, :]
        )
        matched = jnp.sum(basis_weight * second, axis=0)
        weight_f = weights.astype(jnp.float32)
        return ((numer + weight_f * matched, total + weight_f), None)

    start = (
        jnp.zeros((cell_side, cell_side), jnp.float32),
        jnp.ones((cell_side, cell_side), jnp.float32),
    )
    (numer, total), unused = lax.scan(add_visit, start, (padded, ivar_planes, kernel_coef))
    return (numer / total, total)


def solution(mesh):
    placed = (
        P(("celly", "cellx"), None, None),
        P(("celly", "cellx"), None, None),
        P(("celly", "cellx"), None),
        P(("celly", "cellx")),
        P(("celly", "cellx")),
        P(),
        P(),
        P(),
    )
    return jax.shard_map(
        local,
        mesh=mesh,
        in_specs=placed,
        out_specs=(P("celly", "cellx"), P("celly", "cellx")),
        check_vma=False,
    )
```

profile of v0, /device:TPU:29, one launch (start us, length us, event | category | flops | bytes accessed | tf_op | source)
XLA Modules:
  0.0 405.9 jit_solution(4357383674832192790)
XLA Ops:
  4.6 10.6 %all-to-all-start = ((s32[128,2,1]{1,2,0:T(1,128)}), s32[128,2,1]{1,2,0:T(1,128)S(1)}, u32[]{:S(2)}, u32[]{:S(2)}) async-start(s32[128,2,1]{1,2,0:T(1,128)} %bitcast.3), calls=%async_computation | async-start | bytes 131072 | tf_op jit(solution)/shard_map/all_to_all | solution.py:57
  15.2 5.4 %broadcast.86.clone.1 = bf16[256,128,128]{2,1,0:T(8,128)(2,1)} broadcast(bf16[]{:T(256)} %constant.15.clone.1), dimensions={} | broadcast | bytes 8388610 | tf_op jit(solution)/shard_map/broadcast.9
  20.6 19.3 %scatter_fusion.1 = bf16[256,128,128]{2,1,0:T(8,128)(2,1)} fusion(bf16[256,128,128]{2,1,0:T(8,128)(2,1)} %broadcast.86.clone.1, s32[128]{0:T(128)S(1)} %fusion.35, bf16[128,128,128]{2,1,0:T(8,128)(2,1)} %param.10), kind=kCustom, calls=%fused_computation.2 | custom fusion | bytes 12583424 | tf_op jit(solution)/shard_map/scatter | solution.py:48
  39.9 10.2 %all-to-all-start.2 = ((bf16[256,128,128]{2,1,0:T(8,128)(2,1)}), bf16[256,128,128]{2,1,0:T(8,128)(2,1)}, u32[]{:S(2)}, u32[]{:S(2)}) async-start(bf16[256,128,128]{2,1,0:T(8,128)(2,1)} %scatter_fusion.1), calls=%async_computation.2 | async-start | bytes 16777216 | tf_op jit(solution)/shard_map/all_to_all | solution.py:55
  50.1 5.4 %broadcast.86.clone = bf16[256,128,128]{2,1,0:T(8,128)(2,1)} broadcast(bf16[]{:T(256)} %constant.15.clone.1), dimensions={} | broadcast | bytes 8388610 | tf_op jit(solution)/shard_map/broadcast.9
  55.5 19.3 %scatter_fusion = bf16[256,128,128]{2,1,0:T(8,128)(2,1)} fusion(bf16[256,128,128]{2,1,0:T(8,128)(2,1)} %broadcast.86.clone, s32[128]{0:T(128)S(1)} %fusion.35, bf16[128,128,128]{2,1,0:T(8,128)(2,1)} %param.11), kind=kCustom, calls=%fused_computation.1 | custom fusion | bytes 12583424 | tf_op jit(solution)/shard_map/scatter | solution.py:51
  74.8 75.3 %all-to-all-done.2 = bf16[256,128,128]{2,1,0:T(8,128)(2,1)} async-done(((bf16[256,128,128]{2,1,0:T(8,128)(2,1)}), bf16[256,128,128]{2,1,0:T(8,128)(2,1)}, u32[]{:S(2)}, u32[]{:S(2)}) %all-to-all-start.2) | async-done | bytes 8388640 | tf_op jit(solution)/shard_map/all_to_all | solution.py:55
  150.2 13.1 %all-to-all-start.1 = ((bf16[256,128,128]{2,1,0:T(8,128)(2,1)}), bf16[256,128,128]{2,1,0:T(8,128)(2,1)}, u32[]{:S(2)}, u32[]{:S(2)}) async-start(bf16[256,128,128]{2,1,0:T(8,128)(2,1)} %scatter_fusion), calls=%async_computation.1 | async-start | bytes 16777216 | tf_op jit(solution)/shard_map/all_to_all | solution.py:56
  169.9 8.4 %fusion.23 = bf16[10,8,128,128]{3,1,2,0:T(8,128)(2,1)S(1)} fusion(bf16[32,8,128,128]{3,2,1,0:T(8,128)(2,1)} %bitcast.25, s32[256]{0:T(256)S(1)} %eq.60), kind=kOutput, calls=%fused_computation.36 | convolution fusion | flops 672419840 | bytes 11011072 | tf_op jit(solution)/shard_map/dot_general | solution.py:63
  179.0 4.3 %copy.39 = bf16[20,2,128,2,128]{4,3,2,1,0:T(2,128)(2,1)} copy(bf16[20,2,128,2,128]{4,2,3,1,0:T(8,128)(2,1)S(1)} %bitcast.81) | data formatting | bytes 5242880 | tf_op jit(solution)/shard_map/transpose | solution.py:69
  183.3 4.2 %reshape.135 = bf16[20,256,256]{2,1,0:T(8,128)(2,1)S(1)} reshape(bf16[20,2,128,2,128]{4,3,2,1,0:T(2,128)(2,1)} %copy.39) | data formatting | bytes 5242880 | tf_op jit(solution)/shard_map/reshape | solution.py:69
  190.8 15.0 %collective-permute-start = (bf16[20,20,256]{2,1,0:T(8,128)(2,1)}, bf16[20,20,256]{2,1,0:T(8,128)(2,1)}, u32[]{:S(2)}, u32[]{:S(2)}) collective-permute-start(bf16[20,20,256]{2,1,0:T(8,128)(2,1)} %get-tuple-element.175), channel_id=1, source_target_pairs={{0,8},{8,16},{16,24},{24,32},{32,40},{40,48},{48,56},{56,64},{64,7... | collective-permute-start | bytes 614408 | tf_op jit(solution)/shard_map/ppermute | solution.py:12
  205.8 3.9 fusion.28
  210.9 55.5 %collective-permute-done.1 = bf16[20,20,256]{2,1,0:T(8,128)(2,1)S(1)} collective-permute-done((bf16[20,20,256]{2,1,0:T(8,128)(2,1)}, bf16[20,20,256]{2,1,0:T(8,128)(2,1)S(1)}, u32[]{:S(2)}, u32[]{:S(2)}) %collective-permute-start.1) | collective-permute-done | bytes 204832 | tf_op jit(solution)/shard_map/ppermute | solution.py:15
  266.3 7.1 %collective-permute-done = bf16[20,20,256]{2,1,0:T(8,128)(2,1)} collective-permute-done((bf16[20,20,256]{2,1,0:T(8,128)(2,1)}, bf16[20,20,256]{2,1,0:T(8,128)(2,1)}, u32[]{:S(2)}, u32[]{:S(2)}) %collective-permute-start) | collective-permute-done | bytes 204832 | tf_op jit(solution)/shard_map/ppermute | solution.py:12
  286.0 3.0 collective-permute-start.2
  289.0 8.4 %fusion.20 = bf16[10,8,128,128]{3,1,2,0:T(8,128)(2,1)S(1)} fusion(bf16[32,8,128,128]{3,2,1,0:T(8,128)(2,1)} %bitcast.20, s32[256]{0:T(256)S(1)} %eq.60), kind=kOutput, calls=%fused_computation.35 | convolution fusion | flops 672419840 | bytes 11011072 | tf_op jit(solution)/shard_map/dot_general | solution.py:63
  298.2 4.3 %copy.38 = bf16[20,2,128,2,128]{4,3,2,1,0:T(2,128)(2,1)} copy(bf16[20,2,128,2,128]{4,2,3,1,0:T(8,128)(2,1)S(1)} %bitcast.82) | data formatting | bytes 5242880 | tf_op jit(solution)/shard_map/transpose | solution.py:69
  302.4 5.4 %reshape.132 = bf16[20,256,256]{2,1,0:T(8,128)(2,1)} reshape(bf16[20,2,128,2,128]{4,3,2,1,0:T(2,128)(2,1)} %copy.38) | data formatting | bytes 5242880 | tf_op jit(solution)/shard_map/reshape | solution.py:69
  312.9 7.3 %pad_maximum_fusion = bf16[20,296,296]{2,1,0:T(8,128)(2,1)} fusion(bf16[20,296,20]{2,1,0:T(8,128)(2,1)} %copy.43, bf16[20,20,256]{2,1,0:T(8,128)(2,1)S(1)} %collective-permute-done.1, bf16[20,256,256]{2,1,0:T(8,128)(2,1)S(1)} %reshape.135, bf16[20,20,256]{2,1,0:T(8,128)(2,1)} %collective-permute-done, bf16[20,296,20]{2,1,0:T(8,128)(2,1)} %copy.42), kind=kLoop, calls=%fused_computation.33 | loop fusion | flops 17523200 | bytes 7009280 | tf_op jit(solution)/shard_map/concatenate | solution.py:16
  320.3 84.6 %while.13 = (s32[]{:T(128)}, f32[256,256]{1,0:T(8,128)S(1)}, f32[256,256]{1,0:T(8,128)S(1)}, bf16[20,256,256]{2,1,0:T(8,128)(2,1)}, f32[20,7,3]{1,2,0:T(4,128)S(...) while((s32[]{:T(128)}, f32[256,256]{1,0:T(8,128)S(1)}, ...), condition=%wide.region_6.7_spmd.clone, body=%wide.region_4.6_spmd.clone.sunk | while | flops 587839232 | bytes 4086335 | solution.py:105
  320.5 3.0 multiply_reduce_fusion.2
  328.9 3.0 multiply_reduce_fusion.2
  337.4 3.0 multiply_reduce_fusion.2
  345.8 3.0 multiply_reduce_fusion.2
  354.3 3.0 multiply_reduce_fusion.2
  362.8 3.0 multiply_reduce_fusion.2
  371.2 3.0 multiply_reduce_fusion.2
  379.7 3.0 multiply_reduce_fusion.2
  388.2 3.0 multiply_reduce_fusion.2
  392.4 3.0 multiply_reduce_fusion.2
  396.6 3.0 multiply_reduce_fusion.2
  (172 shorter events, 85.6 us)
Async XLA Ops:
  0.6 163.6 %copy-start = (bf16[7,41]{1,0:T(8,128)(2,1)S(1)}, bf16[7,41]{1,0:T(8,128)(2,1)}, u32[]{:S(2)}) copy-start(bf16[7,41]{1,0:T(8,128)(2,1)} %param.15) | copy-start | bytes 1726
  4.6 35.3 %all-to-all-start = ((s32[128,2,1]{1,2,0:T(1,128)}), s32[128,2,1]{1,2,0:T(1,128)S(1)}, u32[]{:S(2)}, u32[]{:S(2)}) async-start(s32[128,2,1]{1,2,0:T(1,128)} %bitcast.3), calls=%async_computation | async-start | bytes 131072 | tf_op jit(solution)/shard_map/all_to_all | solution.py:57
  39.9 110.3 %all-to-all-start.2 = ((bf16[256,128,128]{2,1,0:T(8,128)(2,1)}), bf16[256,128,128]{2,1,0:T(8,128)(2,1)}, u32[]{:S(2)}, u32[]{:S(2)}) async-start(bf16[256,128,128]{2,1,0:T(8,128)(2,1)} %scatter_fusion.1), calls=%async_computation.2 | async-start | bytes 16777216 | tf_op jit(solution)/shard_map/all_to_all | solution.py:55
  74.8 88.5 %copy-start.4 = (f32[20,7,3]{0,1,2:T(8,128)S(1)}, f32[20,7,3]{0,1,2:T(8,128)}, u32[]{:S(2)}) copy-start(f32[20,7,3]{0,1,2:T(8,128)} %param.17) | copy-start | bytes 5044
  150.2 138.9 %all-to-all-start.1 = ((bf16[256,128,128]{2,1,0:T(8,128)(2,1)}), bf16[256,128,128]{2,1,0:T(8,128)(2,1)}, u32[]{:S(2)}, u32[]{:S(2)}) async-start(bf16[256,128,128]{2,1,0:T(8,128)(2,1)} %scatter_fusion), calls=%async_computation.1 | async-start | bytes 16777216 | tf_op jit(solution)/shard_map/all_to_all | solution.py:56
  163.5 0.7 copy-start.3
  183.3 22.4 %copy-start.5 = (bf16[7,41]{1,0:T(8,128)(2,1)S(1)}, bf16[7,41]{1,0:T(8,128)(2,1)}, u32[]{:S(2)}) copy-start(bf16[7,41]{1,0:T(8,128)(2,1)} %param.16) | copy-start | bytes 1726
  188.4 78.0 %collective-permute-start.1 = (bf16[20,20,256]{2,1,0:T(8,128)(2,1)}, bf16[20,20,256]{2,1,0:T(8,128)(2,1)S(1)}, u32[]{:S(2)}, u32[]{:S(2)}) collective-permute-start(bf16[20,20,256]{2,1,0:T(8,128)(2,1)} %get-tuple-element.176), channel_id=1, source_target_pairs={{8,0},{16,8},{24,16},{32,24},{40,32},{48,40},{56,48},{64,56},{72,6... | collective-permute-start | bytes 614408 | tf_op jit(solution)/shard_map/ppermute | solution.py:15
  190.8 82.6 %collective-permute-start = (bf16[20,20,256]{2,1,0:T(8,128)(2,1)}, bf16[20,20,256]{2,1,0:T(8,128)(2,1)}, u32[]{:S(2)}, u32[]{:S(2)}) collective-permute-start(bf16[20,20,256]{2,1,0:T(8,128)(2,1)} %get-tuple-element.175), channel_id=1, source_target_pairs={{0,8},{8,16},{16,24},{24,32},{32,40},{40,48},{48,56},{56,64},{64,7... | collective-permute-start | bytes 614408 | tf_op jit(solution)/shard_map/ppermute | solution.py:12
  280.9 26.9 %collective-permute-start.3 = (bf16[20,296,20]{1,2,0:T(8,128)(2,1)}, bf16[20,296,20]{1,2,0:T(8,128)(2,1)}, u32[]{:S(2)}, u32[]{:S(2)}) collective-permute-start(bf16[20,296,20]{1,2,0:T(8,128)(2,1)} %copy.41), channel_id=1, source_target_pairs={{1,0},{2,1},{3,2},{4,3},{5,4},{6,5},{7,6},{9,8},{10,9},{11,10},{12... | collective-permute-start | bytes 710408 | tf_op jit(solution)/shard_map/ppermute | solution.py:15
  286.0 24.4 %collective-permute-start.2 = (bf16[20,296,20]{1,2,0:T(8,128)(2,1)}, bf16[20,296,20]{1,2,0:T(8,128)(2,1)}, u32[]{:S(2)}, u32[]{:S(2)}) collective-permute-start(bf16[20,296,20]{1,2,0:T(8,128)(2,1)} %copy.40), channel_id=1, source_target_pairs={{0,1},{1,2},{2,3},{3,4},{4,5},{5,6},{6,7},{8,9},{9,10},{10,11},{11... | collective-permute-start | bytes 710408 | tf_op jit(solution)/shard_map/ppermute | solution.py:12
  404.9 0.8 copy-start.2
  404.9 0.8 copy-start.1
where the time goes:
time: 413 us; the launch traced here: 406 us
  waiting for transfers between devices  138 us (33%)
  local copies, waits for them, and re-layouts  88.4 us (21%)
  matrix products  83.6 us (20%)
  starting transfers between devices  56.9 us (14%)
  other arithmetic  37.1 us (9%)
    all_to_all x1, waiting for transfers between devices, local(): lax.all_to_all(send_flux, ('celly', 'cellx'), split_axis=0, concat_axis=0...  75.3 us
    dot_general x20, matrix products, add_visit(): jnp.einsum('biq,bkq->bik', first, col_table, preferred_element_type=jnp.f...  59.9 us
    ppermute x2, waiting for transfers between devices, padded_2(): lax.ppermute(lax.slice_in_dim(block, 0, width, axis=dim), axis, backward)  55.5 us
    scatter x2, local copies, waits for them, and re-layouts, local(): jnp.zeros((slots_all, block_side, block_side), jnp.bfloat16).at[target]  38.7 us
    add x20, other arithmetic, add_visit(): return ((numer + weight_f * matched, total + weight_f), None)  20.3 us
    ppermute x2, starting transfers between devices, padded_2(): lax.ppermute(lax.slice_in_dim(block, block.shape[dim] - width, None, axis...  18 us
    dot_general x2, matrix products, place(): jnp.dot(picker, received.reshape(slots_all, block_side * block_side), pre...  16.8 us
    all_to_all x1, starting transfers between devices, local(): lax.all_to_all(send_ivar, ('celly', 'cellx'), split_axis=0, concat_axis=0...  13.1 us
  transfers between devices with their start and end apart: 7, of which 3 were waited for; matrix products, arithmetic and copies ran while one was open for 27% of the time, Pallas kernels for 0%

commit v1 on v0

v1 whole, which is shorter than its diff:
```python
import functools

import jax
import jax.numpy as jnp
from jax import lax
from jax.experimental import pallas as pl
from jax.experimental.pallas import tpu as pltpu
from jax.sharding import PartitionSpec as P

MESH = pl.DeviceIdType.MESH
SIDE = 4
CHIPS = SIDE**3
EDGE = 32
GROUP = 4


def toeplitz_tables(taps, count, offsets):
    half = (taps.shape[1] - 1) // 2
    index = offsets[None, :] + half - jnp.arange(count)[:, None]
    picker = (index[:, :, None] == jnp.arange(taps.shape[1])).astype(jnp.float32)
    return jnp.einsum("ijp,bp->bij", picker, taps.astype(jnp.float32)).astype(jnp.bfloat16)


def coordinates():
    row, col = lax.axis_index("celly"), lax.axis_index("cellx")
    return [row // SIDE, row % SIDE, col // 2, col % 2]


def device(q):
    return (q[0] * SIDE + q[1], q[2] * 2 + q[3])


def shifted(q, axis, d, n=SIDE):
    r = list(q)
    r[axis] = lax.rem(q[axis] + d, n)
    return r


def gather_kernel(index_ref, flux_ref, ivar_ref, out_ref):
    arr = pl.program_id(0)
    step = pl.program_id(1)
    per = out_ref.shape[0]

    def pick(ref):
        def body(i, carry):
            out_ref[i] = ref[index_ref[step * per + i]]
            return carry

        lax.fori_loop(0, per, body, 0)

    pl.when(arr == 0)(lambda: pick(flux_ref))
    pl.when(arr == 1)(lambda: pick(ivar_ref))


def units_of(slots):
    units = [(s, 0, 128, s) for s in range(3)]
    if slots == 4:
        units += [(3, 0, 48, 0), (3, 48, 48, 1), (3, 96, 32, 2)]
    return units


def route_kernel(
    slots, visits, bases,
    order_ref, fresh_ref, last_ref, has_ref, coef_ref, t0, rowt_ref, colt_ref,
    numer_out, total_out, t1, t2,
    t_flux, t_ivar, seg, win, matched, strips, got,
    s1, r1, s2, r2, s3, r3, s4, r4, ls, hs, hr,
):
    t = (t_flux, t_ivar)
    q = coordinates()
    row, col = lax.axis_index("celly"), lax.axis_index("cellx")
    rows_n, cols_n = lax.axis_size("celly"), lax.axis_size("cellx")
    units = units_of(slots)
    count = len(units)
    partner = shifted(q, 3, 1, 2)
    above = (lax.rem(row + rows_n - 1, rows_n), col)
    below = (lax.rem(row + 1, rows_n), col)
    left = (row, lax.rem(col + cols_n - 1, cols_n))
    right = (row, lax.rem(col + 1, cols_n))

    barrier = pltpu.get_barrier_semaphore()
    peers = [device(shifted(q, a, d)) for a in range(3) for d in (1, 2, 3)]
    peers += [device(partner), above, below, left, right]
    for peer in peers:
        pl.semaphore_signal(barrier, inc=1, device_id=peer, device_id_type=MESH)
    pl.semaphore_wait(barrier, len(peers))

    def remote(src, dst, send, recv, to):
        return pltpu.make_async_remote_copy(
            src, dst, send, recv, device_id=to, device_id_type=MESH
        )

    def at(ref, unit, lead, where):
        slot, start, rows, _ = units[unit]
        index = [where.get(axis, slice(None)) for axis in range(3)]
        return ref.at[(*lead, slot, *index, pl.ds(start, rows))]

    def axes(unit):
        a = units[unit][3]
        return a, (a + 1) % 3, (a + 2) % 3

    def first_hop(arr, u, d):
        a, b, c = axes(u)
        to = shifted(q, a, d)
        return remote(
            at(t0, u, (arr,), {a: to[a]}), at(t1, u, (arr,), {a: q[a]}),
            s1.at[arr, u, d], r1.at[arr, u, q[a]], device(to),
        )

    def first_arrival(arr, u, da):
        a, b, c = axes(u)
        asrc = lax.rem(q[a] + da, SIDE)
        place = at(t1, u, (arr,), {a: asrc})
        return remote(place, place, s1.at[arr, u, da], r1.at[arr, u, asrc], device(q))

    def second_hop(arr, u, da, d):
        a, b, c = axes(u)
        to = shifted(q, b, d)
        asrc = lax.rem(q[a] + da, SIDE)
        return remote(
            at(t0 if da == 0 else t1, u, (arr,), {a: asrc, b: to[b]}),
            at(t2, u, (arr,), {a: asrc, b: q[b]}),
            s2.at[arr, u, d, da], r2.at[arr, u, q[b], asrc], device(to),
        )

    def second_arrival(arr, u, db, da):
        a, b, c = axes(u)
        asrc = lax.rem(q[a] + da, SIDE)
        bsrc = lax.rem(q[b] + db, SIDE)
        place = at(t2, u, (arr,), {a: asrc, b: bsrc})
        return remote(place, place, s2.at[arr, u, db, da], r2.at[arr, u, bsrc, asrc], device(q))

    def third_sources(arr, u, db, cc):
        a, b, c = axes(u)
        bsrc = lax.rem(q[b] + db, SIDE)
        if db:
            return [(at(t2, u, (arr,), {b: bsrc, c: cc}), {b: bsrc, c: q[c]})]
        pairs = []
        for da in range(SIDE):
            asrc = lax.rem(q[a] + da, SIDE)
            source = at(t0 if da == 0 else t1, u, (arr,), {a: asrc, b: bsrc, c: cc})
            pairs.append((source, {a: asrc, b: bsrc, c: q[c]}))
        return pairs

    def third_hop(arr, u, db, d):
        a, b, c = axes(u)
        to = shifted(q, c, d)
        bsrc = lax.rem(q[b] + db, SIDE)
        return [
            remote(source, at(t[arr], u, (0,), where), s3.at[arr, u, d, db], r3.at[arr, u, q[c], bsrc], device(to))
            for source, where in third_sources(arr, u, db, to[c])
        ]

    def third_whole(arr, u, db, d):
        a, b, c = axes(u)
        bsrc = lax.rem(q[b] + db, SIDE)
        csrc = lax.rem(q[c] + d, SIDE)
        place = at(t[arr], u, (0,), {b: bsrc, c: csrc})
        return remote(place, place, s3.at[arr, u, d, db], r3.at[arr, u, csrc, bsrc], device(q))

    def third_stay(arr, u, db):
        a, b, c = axes(u)
        return [
            pltpu.make_async_copy(source, at(t[arr], u, (0,), where), ls.at[arr, u, db])
            for source, where in third_sources(arr, u, db, q[c])
        ]

    def stay_whole(arr, u, db):
        a, b, c = axes(u)
        place = at(t[arr], u, (0,), {b: lax.rem(q[b] + db, SIDE), c: q[c]})
        return pltpu.make_async_copy(place, place, ls.at[arr, u, db])

    def fourth_hop(arr, u, dc):
        a, b, c = axes(u)
        csrc = lax.rem(q[c] + dc, SIDE)
        return remote(
            at(t[arr], u, (0,), {c: csrc}), at(t[arr], u, (1,), {c: csrc}),
            s4.at[arr, u, dc], r4.at[arr, u, csrc], device(partner),
        )

    def stage1(arr):
        for d in (2, 1, 3):
            for u in range(count):
                first_hop(arr, u, d).start()

    def stage2(arr):
        for da in (0, 1, 3, 2):
            for u in range(count):
                if da:
                    first_arrival(arr, u, da).wait_recv()
                for d in (2, 1, 3):
                    second_hop(arr, u, da, d).start()

    def stage3(arr):
        for db in (0, 1, 3, 2):
            for u in range(count):
                if db:
                    for da in range(SIDE):
                        second_arrival(arr, u, db, da).wait_recv()
                for d in (2, 1, 3):
                    for copy in third_hop(arr, u, db, d):
                        copy.start()
                for copy in third_stay(arr, u, db):
                    copy.start()

    def stage4(arr):
        for dc in (0, 1, 3, 2):
            for u in range(count):
                for db in range(SIDE):
                    if dc:
                        third_whole(arr, u, db, dc).wait_recv()
                    else:
                        stay_whole(arr, u, db).wait()
                fourth_hop(arr, u, dc).start()
        for dc in (0, 1, 3, 2):
            for u in range(count):
                fourth_hop(arr, u, dc).wait()

    def drain(arr):
        for u in range(count):
            for d in (1, 2, 3):
                first_hop(arr, u, d).wait_send()
                for e in range(SIDE):
                    second_hop(arr, u, e, d).wait_send()
                    third_whole(arr, u, e, d).wait_send()

    def segments(arr):
        def body(p, total):
            i = order_ref[p]
            block = t[arr][i // (CHIPS * slots), (i // CHIPS) % slots,
                      (i // 16) % 4, (i // 4) % 4, i % 4].astype(jnp.float32)
            total = jnp.where(fresh_ref[p] > 0, block, total + block)
            seg[p] = total.astype(jnp.bfloat16)
            return total

        lax.fori_loop(0, seg.shape[0], body, jnp.zeros((128, 128), jnp.float32))

    def summed(key):
        block = seg[last_ref[key]]
        return jnp.where(has_ref[key] > 0, block, jnp.zeros_like(block))

    def place_flux():
        def body(v, carry):
            for sr in range(2):
                for sc in range(2):
                    win[v, 128 * sr : 128 * sr + 128, 128 * sc : 128 * sc + 128] = summed(
                        v * 4 + sr * 2 + sc
                    )
            return carry

        lax.fori_loop(0, visits, body, 0)

    down = remote(
        win.at[:, pl.ds(256 - EDGE, EDGE), pl.ds(0, 256)],
        win.at[:, pl.ds(256, EDGE), pl.ds(0, 256)],
        hs.at[0], hr.at[0], below,
    )
    up = remote(
        win.at[:, pl.ds(0, EDGE), pl.ds(0, 256)],
        win.at[:, pl.ds(256 + EDGE, EDGE), pl.ds(0, 256)],
        hs.at[1], hr.at[1], above,
    )
    to_right = remote(strips.at[0], got.at[0], hs.at[2], hr.at[2], right)
    to_left = remote(strips.at[1], got.at[1], hs.at[3], hr.at[3], left)

    def pack_columns():
        top_ok = (row > 0).astype(jnp.float32)
        bottom_ok = (row < rows_n - 1).astype(jnp.float32)

        def clear(v, carry):
            lo = win[v, 256 : 256 + EDGE, 0:256].astype(jnp.float32) * top_ok
            hi = win[v, 256 + EDGE : 256 + 2 * EDGE, 0:256].astype(jnp.float32) * bottom_ok
            win[v, 256 : 256 + EDGE, 0:256] = lo.astype(jnp.bfloat16)
            win[v, 256 + EDGE : 256 + 2 * EDGE, 0:256] = hi.astype(jnp.bfloat16)
            return carry

        lax.fori_loop(0, visits, clear, 0)
        lane = lax.broadcasted_iota(jnp.int32, (256 + 2 * EDGE, 128), 1)

        def body(g, carry):
            ends = jnp.zeros(lane.shape, jnp.float32)
            starts = jnp.zeros(lane.shape, jnp.float32)
            for k in range(GROUP):
                mine = (lane >= EDGE * k) & (lane < EDGE * k + EDGE)
                tail = win[g * GROUP + k, :, 128:256].astype(jnp.float32)
                head = win[g * GROUP + k, :, 0:128].astype(jnp.float32)
                ends = jnp.where(mine, pltpu.roll(tail, (EDGE * k + EDGE) % 128, 1), ends)
                starts = jnp.where(mine, pltpu.roll(head, EDGE * k, 1) if k else head, starts)
            strips[0, g] = ends.astype(jnp.bfloat16)
            strips[1, g] = starts.astype(jnp.bfloat16)
            return carry

        lax.fori_loop(0, visits // GROUP, body, 0)

    def unpack_columns():
        left_ok = (col > 0).astype(jnp.float32)
        right_ok = (col < cols_n - 1).astype(jnp.float32)
        lane = lax.broadcasted_iota(jnp.int32, (256 + 2 * EDGE, 128), 1)

        def body(g, carry):
            lefts = got[0, g].astype(jnp.float32) * left_ok
            rights = got[1, g].astype(jnp.float32) * right_ok
            for k in range(GROUP):
                lo = pltpu.roll(lefts, (128 - EDGE * k) % 128, 1) if k else lefts
                hi = pltpu.roll(rights, (128 + EDGE - EDGE * k) % 128, 1) if k != 1 else rights
                tile = jnp.where(lane < EDGE, lo, jnp.where(lane < 2 * EDGE, hi, 0.0))
                win[g * GROUP + k, :, 256:384] = tile.astype(jnp.bfloat16)
            return carry

        lax.fori_loop(0, visits // GROUP, body, 0)

    def position(index, axis, size):
        pixel = (index * 256 + lax.broadcasted_iota(jnp.int32, (256, 256), axis)).astype(jnp.float32)
        return (pixel + 0.5) * (2.0 / (256 * size)) - 1.0

    def correlate(start, stop):
        def body(v, carry):
            rows_pos = position(row, 0, rows_n)
            cols_pos = position(col, 1, cols_n)
            window = win[v]
            acc = jnp.zeros((256, 256), jnp.float32)
            for b in range(bases):
                first = jnp.dot(rowt_ref[b], window, preferred_element_type=jnp.float32)
                second = jnp.dot(
                    first.astype(jnp.bfloat16), colt_ref[b], preferred_element_type=jnp.float32
                )
                weight = coef_ref[v, b * 3] + coef_ref[v, b * 3 + 1] * rows_pos
                acc += (weight + coef_ref[v, b * 3 + 2] * cols_pos) * second
            matched[v] = acc
            return carry

        lax.fori_loop(start, stop, body, 0)

    def combine():
        for sr in range(2):
            for sc in range(2):
                rows, cols = slice(128 * sr, 128 * sr + 128), slice(128 * sc, 128 * sc + 128)

                def body(v, carry, rows=rows, cols=cols, quarter=sr * 2 + sc):
                    numer, total = carry
                    weight = summed(v * 4 + quarter).astype(jnp.float32)
                    return numer + weight * matched[v, rows, cols], total + weight

                zero = jnp.zeros((128, 128), jnp.float32)
                numer, total = lax.fori_loop(0, visits, body, (zero, zero + 1.0))
                numer_out[rows, cols] = numer / total
                total_out[rows, cols] = total

    stage1(0)
    stage2(0)
    stage3(0)
    stage1(1)
    stage4(0)
    segments(0)
    place_flux()
    down.start()
    up.start()
    stage2(1)
    down.wait()
    up.wait()
    pack_columns()
    to_right.start()
    to_left.start()
    to_right.wait()
    to_left.wait()
    unpack_columns()
    correlate(0, visits // 2)
    stage3(1)
    correlate(visits // 2, visits)
    stage4(1)
    segments(1)
    combine()
    drain(0)
    drain(1)


def route(slots, collective, order, fresh, last, has, coef, send, row_table, col_table):
    visits, bases = coef.shape[0], row_table.shape[0]
    count = len(units_of(slots))
    dma = pltpu.SemaphoreType.DMA
    hop = jax.ShapeDtypeStruct((2, slots, 4, 4, 4, 128, 128), jnp.bfloat16)
    image = jax.ShapeDtypeStruct((256, 256), jnp.float32)
    smem = pl.BlockSpec(memory_space=pltpu.SMEM)
    vmem = pl.BlockSpec(memory_space=pltpu.VMEM)
    anywhere = pl.BlockSpec(memory_space=pl.ANY)
    coadd, weight, _, _ = pl.pallas_call(
        functools.partial(route_kernel, slots, visits, bases),
        out_shape=[image, image, hop, hop],
        in_specs=[smem] * 5 + [anywhere] + [vmem] * 2,
        out_specs=[vmem] * 2 + [anywhere] * 2,
        scratch_shapes=[
            pltpu.VMEM((2, slots, 4, 4, 4, 128, 128), jnp.bfloat16),
            pltpu.VMEM((2, slots, 4, 4, 4, 128, 128), jnp.bfloat16),
            pltpu.VMEM((256, 128, 128), jnp.bfloat16),
            pltpu.VMEM((visits, 256 + 2 * EDGE, 384), jnp.bfloat16),
            pltpu.VMEM((visits, 256, 256), jnp.float32),
            pltpu.VMEM((2, visits // GROUP, 256 + 2 * EDGE, 128), jnp.bfloat16),
            pltpu.VMEM((2, visits // GROUP, 256 + 2 * EDGE, 128), jnp.bfloat16),
            dma((2, count, 4)), dma((2, count, 4)),
            dma((2, count, 4, 4)), dma((2, count, 4, 4)),
            dma((2, count, 4, 4)), dma((2, count, 4, 4)),
            dma((2, count, 4)), dma((2, count, 4)),
            dma((2, count, 4)), dma((4,)), dma((4,)),
        ],
        compiler_params=pltpu.CompilerParams(
            collective_id=collective, has_side_effects=True, vmem_limit_bytes=63 * 2**20
        ),
    )(order, fresh, last, has, coef, send, row_table, col_table)
    return coadd, weight


def local(flux_blocks, ivar_blocks, dest_cell, visit_id, slot_id, row_taps, col_taps, kernel_coef):
    slots = 4
    blocks = flux_blocks.shape[0]
    visits, bases = kernel_coef.shape[:2]
    bins = visits * 4
    me_row, me_col = lax.axis_index("celly"), lax.axis_index("cellx")
    my_chip, my_core = me_row * 4 + me_col // 2, me_col % 2

    target = dest_cell[:, 0]
    chip = target // 2
    i = jnp.arange(blocks)
    rank = jnp.sum((chip[:, None] == chip[None, :]) & (i[None, :] < i[:, None]), axis=1)
    spot = rank * CHIPS + chip
    hit = spot[None, :] == jnp.arange(slots * CHIPS)[:, None]
    index = jnp.sum(jnp.where(hit, i[None, :], 0), axis=1).astype(jnp.int32)
    code = (target % 2) * bins + visit_id * 4 + slot_id
    tags = jnp.sum(jnp.where(hit, code[None, :] + 1, 0), axis=1) - 1
    tags = lax.all_gather(tags.astype(jnp.int32), ("celly", "cellx"), axis=0, tiled=False)

    def gathered(number):
        per = 32
        return pl.pallas_call(
            gather_kernel,
            out_shape=jax.ShapeDtypeStruct((2, number, CHIPS, 128, 128), jnp.bfloat16),
            grid_spec=pltpu.PrefetchScalarGridSpec(
                num_scalar_prefetch=1,
                grid=(2, number * CHIPS // per),
                in_specs=[pl.BlockSpec((blocks, 128, 128), lambda a, s, ix: (0, 0, 0))] * 2,
                out_specs=pl.BlockSpec(
                    (None, None, per, 128, 128),
                    lambda a, s, ix: (a, s // (CHIPS // per), s % (CHIPS // per), 0, 0),
                ),
            ),
            compiler_params=pltpu.CompilerParams(vmem_limit_bytes=40 * 2**20),
        )(index, flux_blocks, ivar_blocks).reshape(2, number, 4, 4, 4, 128, 128)

    mine = lax.dynamic_index_in_dim(
        tags.reshape(CHIPS, 2, slots, CHIPS), my_chip, axis=3, keepdims=False
    )
    lanes = jnp.where(my_core == 0, mine, mine[:, ::-1])
    overflow = jnp.any(tags[:, 3 * CHIPS :] >= 0)

    window = jnp.arange(256)
    edge = jnp.arange(EDGE)
    far = jnp.full((128 - 2 * EDGE,), -1000)
    offsets = jnp.concatenate([window, edge - EDGE, edge + 256])
    row_table = toeplitz_tables(row_taps, 256, offsets)
    col_table = toeplitz_tables(col_taps, 256, jnp.concatenate([offsets, far])).transpose(0, 2, 1)
    coef = kernel_coef.reshape(visits, bases * 3)

    def run(number, collective):
        keys = jnp.transpose(lanes[:, :, :number], (1, 2, 0)).reshape(-1) - my_core * bins
        total = keys.shape[0]
        keys = jnp.where((keys >= 0) & (keys < bins), keys, bins)
        order_key = keys * total + jnp.arange(total)
        rank_of = jnp.sum((order_key[None, :] < order_key[:, None]).astype(jnp.int32), axis=1)
        spots = jnp.arange(256)
        order = jnp.sum(
            jnp.where(rank_of[None, :] == spots[:, None], jnp.arange(total)[None, :], 0), axis=1
        ).astype(jnp.int32)
        bin_ids = jnp.arange(bins)
        upto = jnp.sum((keys[None, :] <= bin_ids[:, None]).astype(jnp.int32), axis=1)
        below = jnp.sum((keys[None, :] < bin_ids[:, None]).astype(jnp.int32), axis=1)
        has = (upto > below).astype(jnp.int32)
        fresh = jnp.any(
            (below[None, :] == spots[:, None]) & (has[None, :] > 0), axis=1
        ).astype(jnp.int32)
        last = jnp.maximum(upto - 1, 0).astype(jnp.int32)
        return route(
            number, collective, order, fresh, last, has, coef, gathered(number),
            row_table, col_table,
        )

    return lax.cond(overflow, lambda: run(4, 1), lambda: run(3, 0))


def solution(mesh):
    placed = (
        P(("celly", "cellx"), None, None),
        P(("celly", "cellx"), None, None),
        P(("celly", "cellx"), None),
        P(("celly", "cellx")),
        P(("celly", "cellx")),
        P(),
        P(),
        P(),
    )
    return jax.shard_map(
        local,
        mesh=mesh,
        in_specs=placed,
        out_specs=(P("celly", "cellx"), P("celly", "cellx")),
        check_vma=False,
    )
```

time: 413 us -> 317 us (0.77)
  Pallas kernels: 0 us -> 255 us
  waiting for transfers between devices: 138 us -> 0 us
  local copies, waits for them, and re-layouts: 88.4 us -> 7.11 us
  matrix products: 83.6 us -> 7.55 us
  starting transfers between devices: 56.9 us -> 0 us
  blocking collectives: 0 us -> 35.7 us
  other arithmetic: 37.1 us -> 5.92 us
    pallas_call x0 -> x2, Pallas kernels: none -> 255 us  [the longest x1 241 us: route(): pl.pallas_call(functools.partial(route_kernel, slots, visits, bases), out...]
    dot_general x22 -> x0, matrix products: 76.8 us -> none  [the longest x20 59.9 us: add_visit(): jnp.einsum('biq,bkq->bik', first, col_table, preferred_element_type=jnp.f...]
    all_to_all x3 -> x0, waiting for transfers between devices: 75.3 us -> none  [the longest x1 75.3 us: local(): lax.all_to_all(send_flux, ('celly', 'cellx'), split_axis=0, concat_axis=0...]
    ppermute x4 -> x0, waiting for transfers between devices: 62.5 us -> none  [the longest x2 55.5 us: padded_2(): lax.ppermute(lax.slice_in_dim(block, 0, width, axis=dim), axis, backward)]
    scatter x3 -> x0, local copies, waits for them, and re-layouts: 39.6 us -> none  [the longest x2 38.7 us: local(): jnp.zeros((slots_all, block_side, block_side), jnp.bfloat16).at[target]]
    all_gather x0 -> x1, blocking collectives: none -> 35.7 us  [local(): lax.all_gather(tags.astype(jnp.int32), ('celly', 'cellx'), axis=0, tiled=...]
    all_to_all x3 -> x0, starting transfers between devices: 33.9 us -> none  [the longest x1 13.1 us: local(): lax.all_to_all(send_ivar, ('celly', 'cellx'), split_axis=0, concat_axis=0...]
    ppermute x4 -> x0, starting transfers between devices: 22.9 us -> none  [the longest x2 18 us: padded_2(): lax.ppermute(lax.slice_in_dim(block, block.shape[dim] - width, None, axis...]
  transfers between devices with their start and end apart: 7 -> 0, of which waited for: 3 -> 0; matrix products, arithmetic and copies ran while one was open for 27% -> 0% of each run, Pallas kernels for 0% -> 0%
where the time goes in v1:
time: 317 us; the launch traced here: 314 us
  Pallas kernels  255 us (80%)
  blocking collectives  35.7 us (11%)
  matrix products  7.55 us (2%)
  local copies, waits for them, and re-layouts  7.11 us (2%)
  other arithmetic  5.92 us (2%)
    pallas_call x1, Pallas kernels, route(): pl.pallas_call(functools.partial(route_kernel, slots, visits, bases), out...  241 us
    all_gather x1, blocking collectives, local(): lax.all_gather(tags.astype(jnp.int32), ('celly', 'cellx'), axis=0, tiled=...  35.7 us
    pallas_call x1, Pallas kernels, gathered(): pl.pallas_call(gather_kernel, out_shape=jax.ShapeDtypeStruct((2, number,...  14.4 us
    dot_general x2, matrix products, toeplitz_tables(): jnp.einsum('ijp,bp->bij', picker, taps.astype(jnp.float32))  7.55 us

profile of v1, /device:TPU:29, one launch (start us, length us, event | category | flops | bytes accessed | tf_op | source)
XLA Modules:
  0.0 313.9 jit_solution(5059699205527974371)
XLA Ops:
  0.7 0.7 fusion.19
  1.3 0.7 fusion.20
  2.1 0.2 convert_reduce_fusion.6
  2.2 0.2 select_reduce_fusion.2
  2.4 0.1 add_add_fusion.1
  2.5 0.1 add_add_fusion
  2.6 0.7 copy.39
  3.3 35.7 %all-gather.1 = s32[128,1,256]{2,1,0:T(1,128)S(1)} all-gather(s32[1,1,256]{2,1,0:T(1,128)S(1)} %bitcast.44), channel_id=2, replica_groups=mesh['celly'=16,'cellx'=8] {'celly','cellx'}, dimensions={0}, use_global_device_ids=true | all-gather | bytes 132096 | tf_op jit(solution)/shard_map/all_gather | solution.py:429
  39.0 0.3 reduce
  39.4 0.7 fusion.13
  40.7 0.2 reshape.232
  40.9 0.2 constant_dynamic-slice_fusion
  41.1 0.1 copy.38
  41.2 0.1 iota_subtract_fusion.1
  41.4 3.8 %fusion.11 = bf16[7,256,320]{1,0,2:T(8,128)(2,1)S(1)} fusion(s32[256,320]{0,1:T(8,128)S(1)} %iota_subtract_fusion.1, bf16[7,41]{1,0:T(8,128)(2,1)} %param.15), kind=kOutput, calls=%fused_computation.41 | convolution fusion | flops 50954240 | bytes 1475134 | tf_op jit(solution)/shard_map/ijp,bp->bij/dot_general | solution.py:21
  45.2 3.7 %fusion.10 = bf16[7,384,256]{1,0,2:T(8,128)(2,1)S(1)} fusion(s32[256,384]{1,0:T(8,128)S(1)} %iota_subtract_fusion, bf16[7,41]{1,0:T(8,128)(2,1)S(1)} %copy-done), kind=kOutput, calls=%fused_computation.40 | convolution fusion | flops 61145088 | bytes 1770046 | tf_op jit(solution)/shard_map/ijp,bp->bij/dot_general | solution.py:21
  49.0 263.5 %conditional.1 = (f32[256,256]{1,0:T(8,128)S(1)}, f32[256,256]{1,0:T(8,128)S(1)}) conditional(s32[]{:T(128)} %convert_element_type.54, (s32[64,2,4]{0,2,1:T(4,128)S(1)}, s32[]{:T(128)}, s32[256]{0:T(256)S(1)}, bf16[128,128,128]{2,1,0:T(8,128)(2,1)}, bf16[128,128,128]{2,1,0:T(8,128)(2,1)}, /*index=5*/f32[20,21]{0,1:T(8,128)S(1)}, ...), branch_computations={%region_4.10_spmd, %region_10.16_spmd} | conditional | flops 1489905 | bytes 55403516 | solution.py:485
  49.4 1.9 copy.45.colt_ref
  51.2 0.1 sub.95
  51.3 0.1 convert_reduce_fusion.4
  51.5 0.5 add_maximum_fusion.1.last_ref
  52.0 0.6 broadcast_compare_fusion.1
  52.6 0.1 fusion.3
  52.7 0.5 convert_element_type.46.fresh_ref
  53.2 0.2 convert_reduce_fusion.3
  53.5 0.7 select_reduce_fusion.1.order_ref
  54.2 0.7 copy.43.coef_ref
  54.9 1.8 copy.44.rowt_ref
  56.7 14.4 %branch_1_fun.2 = bf16[2,4,64,128,128]{4,3,2,1,0:T(8,128)(2,1)} custom-call(s32[256]{0:T(256)S(1)} %get-tuple-element.45.index_ref, bf16[128,128,128]{2,1,0:T(8,128)(2,1)} %get-tuple-element.46.flux_ref, bf16[128,128,128]{2,1,0:T(8,128)(2,1)} %get-tuple-element.47.ivar_ref), custom_call_target="tpu_custom_call" | custom-call | tf_op jit(solution)/shard_map/cond/branch_1_fun/pallas_call | solution.py:433
  71.0 241.1 %branch_1_fun.3 = (f32[256,256]{1,0:T(8,128)S(1)}, f32[256,256]{1,0:T(8,128)S(1)}, bf16[2,4,4,4,4,128,128]{6,5,4,3,2,1,0:T(8,128)(2,1)}, bf16[2,4,4,4,4,128,128]{6,5,4,3,2,1,0:T(8,128)(2,1)}) custom-call(s32[256]{0:T(256)} %select_reduce_fusion.1.order_ref, s32[256]{0:T(256)} %convert_element_type.46.fresh_ref, s32[80]{0:T(128)} %add_maximum_fusion.1.last_ref, ...), custom_call_target="tpu_custom_call" | custom-call | tf_op jit(solution)/shard_map/cond/branch_1_fun/pallas_call | solution.py:386
  312.4 0.7 copy.55
  313.2 0.7 copy.56
  (16 shorter events, 0.1 us)
Async XLA Ops:
  0.6 44.6 %copy-start = (bf16[7,41]{1,0:T(8,128)(2,1)S(1)}, bf16[7,41]{1,0:T(8,128)(2,1)}, u32[]{:S(2)}) copy-start(bf16[7,41]{1,0:T(8,128)(2,1)} %param.16) | copy-start | bytes 1726
  312.4 1.4 copy-start.1

commit v2 on v1

--- a/solution.py
+++ b/solution.py
@@ -14,13 +14,6 @@
 GROUP = 4
 
 
-def toeplitz_tables(taps, count, offsets):
-    half = (taps.shape[1] - 1) // 2
-    index = offsets[None, :] + half - jnp.arange(count)[:, None]
-    picker = (index[:, :, None] == jnp.arange(taps.shape[1])).astype(jnp.float32)
-    return jnp.einsum("ijp,bp->bij", picker, taps.astype(jnp.float32)).astype(jnp.bfloat16)
-
-
 def coordinates():
     row, col = lax.axis_index("celly"), lax.axis_index("cellx")
     return [row // SIDE, row % SIDE, col // 2, col % 2]
@@ -36,20 +29,76 @@
     return r
 
 
-def gather_kernel(index_ref, flux_ref, ivar_ref, out_ref):
-    arr = pl.program_id(0)
-    step = pl.program_id(1)
+def gather_kernel(index_ref, flux_ref, ivar_ref, tag_ref, out_ref, all_ref, send, recv, own):
+    arr, step = pl.program_id(0), pl.program_id(1)
     per = out_ref.shape[0]
+    now = arr * pl.num_programs(1) + step
+    x, y, z, core = q = coordinates()
+    partner = shifted(q, 3, 1, 2)
+    whole = slice(None)
+    hops = [
+        [(0, partner, (x, y, z, core))],
+        [(d, shifted(q, 0, d), (x, y, z)) for d in (1, 2, 3)],
+        [(d, shifted(q, 1, d), (whole, y, z)) for d in (1, 2, 3)],
+        [(d, shifted(q, 2, d), (whole, whole, z)) for d in (1, 2, 3)],
+    ]
+    arrivals = [
+        [(0, (x, y, z, 1 - core))],
+        [(d, (lax.rem(x + SIDE - d, SIDE), y, z)) for d in (1, 2, 3)],
+        [(d, (whole, lax.rem(y + SIDE - d, SIDE), z)) for d in (1, 2, 3)],
+        [(d, (whole, whole, lax.rem(z + SIDE - d, SIDE))) for d in (1, 2, 3)],
+    ]
+
+    def copies(hop):
+        return [
+            pltpu.make_async_remote_copy(
+                tag_ref if hop == 0 else all_ref.at[where], all_ref.at[where],
+                send.at[hop, d], recv.at[hop, d], device_id=device(to), device_id_type=MESH,
+            )
+            for d, to, where in hops[hop]
+        ]
+
+    def begin():
+        barrier = pltpu.get_barrier_semaphore()
+        peers = [device(shifted(q, a, d)) for a in range(3) for d in (1, 2, 3)] + [device(partner)]
+        for peer in peers:
+            pl.semaphore_signal(barrier, inc=1, device_id=peer, device_id_type=MESH)
+        mine = pltpu.make_async_copy(tag_ref, all_ref.at[x, y, z, core], own)
+        mine.start()
+        pl.semaphore_wait(barrier, len(peers))
+        for copy in copies(0):
+            copy.start()
+        mine.wait()
+
+    def advance(hop):
+        for d, where in arrivals[hop]:
+            place = all_ref.at[where]
+            pltpu.make_async_remote_copy(
+                place, place, send.at[hop, d], recv.at[hop, d],
+                device_id=device(partner), device_id_type=MESH,
+            ).wait_recv()
+        if hop < 3:
+            for copy in copies(hop + 1):
+                copy.start()
+        else:
+            for earlier in range(4):
+                for copy in copies(earlier):
+                    copy.wait_send()
+
+    pl.when(now == 0)(begin)
 
     def pick(ref):
         def body(i, carry):
-            out_ref[i] = ref[index_ref[step * per + i]]
-            return carry
-
-        lax.fori_loop(0, per, body, 0)
+            for k in range(4):
+                out_ref[4 * i + k] = ref[index_ref[step * per + 4 * i + k]]
+            return carry
+
+        lax.fori_loop(0, per // 4, body, 0)
 
     pl.when(arr == 0)(lambda: pick(flux_ref))
     pl.when(arr == 1)(lambda: pick(ivar_ref))
+    for hop, moment in enumerate((2, 6, 10, 15)):
+        pl.when(now == moment)(functools.partial(advance, hop))
 
 
 def units_of(slots):
@@ -61,15 +110,17 @@
 
 def route_kernel(
     slots, visits, bases,
-    order_ref, fresh_ref, last_ref, has_ref, coef_ref, t0, rowt_ref, colt_ref,
+    order_ref, fresh_ref, last_ref, has_ref, coef_ref, rtaps_ref, ctaps_ref, t0,
     numer_out, total_out, t1, t2,
-    t_flux, t_ivar, seg, win, matched, strips, got,
+    t_flux, t_ivar, seg, win, matched, strips, got, row_table, col_table, first_ref,
     s1, r1, s2, r2, s3, r3, s4, r4, ls, hs, hr,
 ):
     t = (t_flux, t_ivar)
     q = coordinates()
     row, col = lax.axis_index("celly"), lax.axis_index("cellx")
     rows_n, cols_n = lax.axis_size("celly"), lax.axis_size("cellx")
+    taps = rtaps_ref.shape[1]
+    half = (taps - 1) // 2
     units = units_of(slots)
     count = len(units)
     partner = shifted(q, 3, 1, 2)
@@ -191,8 +242,8 @@
                 for d in (2, 1, 3):
                     second_hop(arr, u, da, d).start()
 
-    def stage3(arr):
-        for db in (0, 1, 3, 2):
+    def stage3(arr, groups=(0, 1, 3, 2)):
+        for db in groups:
             for u in range(count):
                 if db:
                     for da in range(SIDE):
@@ -243,7 +294,7 @@
         def body(v, carry):
             for sr in range(2):
                 for sc in range(2):
-                    win[v, 128 * sr : 128 * sr + 128, 128 * sc : 128 * sc + 128] = summed(
+                    win[v, EDGE + 128 * sr : EDGE + 128 * sr + 128, 128 * sc : 128 * sc + 128] = summed(
                         v * 4 + sr * 2 + sc
                     )
             return carry
@@ -251,12 +302,12 @@
         lax.fori_loop(0, visits, body, 0)
 
     down = remote(
-        win.at[:, pl.ds(256 - EDGE, EDGE), pl.ds(0, 256)],
         win.at[:, pl.ds(256, EDGE), pl.ds(0, 256)],
+        win.at[:, pl.ds(0, EDGE), pl.ds(0, 256)],
         hs.at[0], hr.at[0], below,
     )
     up = remote(
-        win.at[:, pl.ds(0, EDGE), pl.ds(0, 256)],
+        win.at[:, pl.ds(EDGE, EDGE), pl.ds(0, 256)],
         win.at[:, pl.ds(256 + EDGE, EDGE), pl.ds(0, 256)],
         hs.at[1], hr.at[1], above,
     )
@@ -268,9 +319,9 @@
         bottom_ok = (row < rows_n - 1).astype(jnp.float32)
 
         def clear(v, carry):
-            lo = win[v, 256 : 256 + EDGE, 0:256].astype(jnp.float32) * top_ok
+            lo = win[v, 0:EDGE, 0:256].astype(jnp.float32) * top_ok
             hi = win[v, 256 + EDGE : 256 + 2 * EDGE, 0:256].astype(jnp.float32) * bottom_ok
-            win[v, 256 : 256 + EDGE, 0:256] = lo.astype(jnp.bfloat16)
+            win[v, 0:EDGE, 0:256] = lo.astype(jnp.bfloat16)
             win[v, 256 + EDGE : 256 + 2 * EDGE, 0:256] = hi.astype(jnp.bfloat16)
             return carry
 
@@ -313,17 +364,52 @@
         pixel = (index * 256 + lax.broadcasted_iota(jnp.int32, (256, 256), axis)).astype(jnp.float32)
         return (pixel + 0.5) * (2.0 / (256 * size)) - 1.0
 
+    def build_tables():
+        def rows_of(b, carry):
+            shape = (128, 128 + 2 * EDGE)
+            tap = lax.broadcasted_iota(jnp.int32, shape, 1) - lax.broadcasted_iota(jnp.int32, shape, 0)
+            table = jnp.zeros(shape, jnp.float32)
+            for k in range(taps):
+                table = jnp.where(tap == k + EDGE - half, rtaps_ref[b, k], table)
+            row_table[pl.ds(pl.multiple_of(b * 128, 128), 128)] = table.astype(jnp.bfloat16)
+            return carry
+
+        lax.fori_loop(0, bases, rows_of, 0)
+
+        def cols_of(b, carry):
+            for part in range(3):
+                shape = (128, 256)
+                line = lax.broadcasted_iota(jnp.int32, shape, 0)
+                source = line + 128 * part
+                if part == 2:
+                    source = jnp.where(
+                        line < EDGE, line - EDGE, jnp.where(line < 2 * EDGE, line + 256 - EDGE, -1000)
+                    )
+                tap = source - lax.broadcasted_iota(jnp.int32, shape, 1)
+                table = jnp.zeros(shape, jnp.float32)
+                for k in range(taps):
+                    table = jnp.where(tap == k - half, ctaps_ref[b, k], table)
+                col_table[b, 128 * part : 128 * part + 128] = table.astype(jnp.bfloat16)
+            return carry
+
+        lax.fori_loop(0, bases, cols_of, 0)
+
     def correlate(start, stop):
         def body(v, carry):
             rows_pos = position(row, 0, rows_n)
             cols_pos = position(col, 1, cols_n)
-            window = win[v]
+            for h in range(2):
+                first = jnp.dot(
+                    row_table[...], win[v, 128 * h : 128 * h + 128 + 2 * EDGE],
+                    preferred_element_type=jnp.float32,
+                )
+                for b in range(bases):
+                    first_ref[b, 128 * h : 128 * h + 128] = first[128 * b : 128 * b + 128].astype(
+                        jnp.bfloat16
+                    )
             acc = jnp.zeros((256, 256), jnp.float32)
             for b in range(bases):
-                first = jnp.dot(rowt_ref[b], window, preferred_element_type=jnp.float32)
-                second = jnp.dot(
-                    first.astype(jnp.bfloat16), colt_ref[b], preferred_element_type=jnp.float32
-                )
+                second = jnp.dot(first_ref[b], col_table[b], preferred_element_type=jnp.float32)
                 weight = coef_ref[v, b * 3] + coef_ref[v, b * 3 + 1] * rows_pos
                 acc += (weight + coef_ref[v, b * 3 + 2] * cols_pos) * second
             matched[v] = acc
@@ -347,26 +433,30 @@
                 total_out[rows, cols] = total
 
     stage1(0)
+    build_tables()
     stage2(0)
+    stage1(1)
     stage3(0)
-    stage1(1)
+    stage2(1)
+    stage3(1, (0,))
     stage4(0)
     segments(0)
     place_flux()
     down.start()
     up.start()
-    stage2(1)
     down.wait()
     up.wait()
     pack_columns()
     to_right.start()
     to_left.start()
+    stage3(1, (1,))
     to_right.wait()
     to_left.wait()
     unpack_columns()
-    correlate(0, visits // 2)
-    stage3(1)
-    correlate(visits // 2, visits)
+    stage3(1, (3,))
+    correlate(0, 2)
+    stage3(1, (2,))
+    correlate(2, visits)
     stage4(1)
     segments(1)
     combine()
@@ -374,8 +464,8 @@
     drain(1)
 
 
-def route(slots, collective, order, fresh, last, has, coef, send, row_table, col_table):
-    visits, bases = coef.shape[0], row_table.shape[0]
+def route(slots, collective, order, fresh, last, has, coef, send, row_taps, col_taps):
+    visits, bases = coef.shape[0], row_taps.shape[0]
     count = len(units_of(slots))
     dma = pltpu.SemaphoreType.DMA
     hop = jax.ShapeDtypeStruct((2, slots, 4, 4, 4, 128, 128), jnp.bfloat16)
@@ -386,7 +476,7 @@
     coadd, weight, _, _ = pl.pallas_call(
         functools.partial(route_kernel, slots, visits, bases),
         out_shape=[image, image, hop, hop],
-        in_specs=[smem] * 5 + [anywhere] + [vmem] * 2,
+        in_specs=[smem] * 7 + [anywhere],
         out_specs=[vmem] * 2 + [anywhere] * 2,
         scratch_shapes=[
             pltpu.VMEM((2, slots, 4, 4, 4, 128, 128), jnp.bfloat16),
@@ -396,6 +486,9 @@
             pltpu.VMEM((visits, 256, 256), jnp.float32),
             pltpu.VMEM((2, visits // GROUP, 256 + 2 * EDGE, 128), jnp.bfloat16),
             pltpu.VMEM((2, visits // GROUP, 256 + 2 * EDGE, 128), jnp.bfloat16),
+            pltpu.VMEM((bases * 128, 128 + 2 * EDGE), jnp.bfloat16),
+            pltpu.VMEM((bases, 384, 256), jnp.bfloat16),
+            pltpu.VMEM((bases, 256, 384), jnp.bfloat16),
             dma((2, count, 4)), dma((2, count, 4)),
             dma((2, count, 4, 4)), dma((2, count, 4, 4)),
             dma((2, count, 4, 4)), dma((2, count, 4, 4)),
@@ -405,7 +498,7 @@
         compiler_params=pltpu.CompilerParams(
             collective_id=collective, has_side_effects=True, vmem_limit_bytes=63 * 2**20
         ),
-    )(order, fresh, last, has, coef, send, row_table, col_table)
+    )(order, fresh, last, has, coef, row_taps, col_taps, send)
     return coadd, weight
 
 
@@ -426,24 +519,40 @@
     index = jnp.sum(jnp.where(hit, i[None, :], 0), axis=1).astype(jnp.int32)
     code = (target % 2) * bins + visit_id * 4 + slot_id
     tags = jnp.sum(jnp.where(hit, code[None, :] + 1, 0), axis=1) - 1
-    tags = lax.all_gather(tags.astype(jnp.int32), ("celly", "cellx"), axis=0, tiled=False)
-
-    def gathered(number):
-        per = 32
-        return pl.pallas_call(
-            gather_kernel,
-            out_shape=jax.ShapeDtypeStruct((2, number, CHIPS, 128, 128), jnp.bfloat16),
-            grid_spec=pltpu.PrefetchScalarGridSpec(
-                num_scalar_prefetch=1,
-                grid=(2, number * CHIPS // per),
-                in_specs=[pl.BlockSpec((blocks, 128, 128), lambda a, s, ix: (0, 0, 0))] * 2,
-                out_specs=pl.BlockSpec(
+    tags = jnp.zeros((8, 128), jnp.int32).at[: slots * CHIPS // 128].set(
+        tags.astype(jnp.int32).reshape(-1, 128)
+    )
+    per = 32
+    send, tags = pl.pallas_call(
+        gather_kernel,
+        out_shape=[
+            jax.ShapeDtypeStruct((2, slots, CHIPS, 128, 128), jnp.bfloat16),
+            jax.ShapeDtypeStruct((4, 4, 4, 2, 8, 128), jnp.int32),
+        ],
+        grid_spec=pltpu.PrefetchScalarGridSpec(
+            num_scalar_prefetch=1,
+            grid=(2, slots * CHIPS // per),
+            in_specs=[pl.BlockSpec((blocks, 128, 128), lambda a, s, ix: (0, 0, 0))] * 2
+            + [pl.BlockSpec(memory_space=pltpu.VMEM)],
+            out_specs=[
+                pl.BlockSpec(
                     (None, None, per, 128, 128),
                     lambda a, s, ix: (a, s // (CHIPS // per), s % (CHIPS // per), 0, 0),
                 ),
-            ),
-            compiler_params=pltpu.CompilerParams(vmem_limit_bytes=40 * 2**20),
-        )(index, flux_blocks, ivar_blocks).reshape(2, number, 4, 4, 4, 128, 128)
+                pl.BlockSpec(memory_space=pl.ANY),
+            ],
+            scratch_shapes=[
+                pltpu.SemaphoreType.DMA((4, 4)),
+                pltpu.SemaphoreType.DMA((4, 4)),
+                pltpu.SemaphoreType.DMA,
+            ],
+        ),
+        compiler_params=pltpu.CompilerParams(
+            collective_id=2, has_side_effects=True, vmem_limit_bytes=40 * 2**20
+        ),
+    )(index, flux_blocks, ivar_blocks, tags)
+    send = send.reshape(2, slots, 4, 4, 4, 128, 128)
+    tags = tags[:, :, :, :, : slots * CHIPS // 128].reshape(2 * CHIPS, slots * CHIPS)
 
     mine = lax.dynamic_index_in_dim(
         tags.reshape(CHIPS, 2, slots, CHIPS), my_chip, axis=3, keepdims=False
@@ -451,12 +560,7 @@
     lanes = jnp.where(my_core == 0, mine, mine[:, ::-1])
     overflow = jnp.any(tags[:, 3 * CHIPS :] >= 0)
 
-    window = jnp.arange(256)
-    edge = jnp.arange(EDGE)
-    far = jnp.full((128 - 2 * EDGE,), -1000)
-    offsets = jnp.concatenate([window, edge - EDGE, edge + 256])
-    row_table = toeplitz_tables(row_taps, 256, offsets)
-    col_table = toeplitz_tables(col_taps, 256, jnp.concatenate([offsets, far])).transpose(0, 2, 1)
+    row_taps_f, col_taps_f = row_taps.astype(jnp.float32), col_taps.astype(jnp.float32)
     coef = kernel_coef.reshape(visits, bases * 3)
 
     def run(number, collective):
@@ -478,8 +582,7 @@
         ).astype(jnp.int32)
         last = jnp.maximum(upto - 1, 0).astype(jnp.int32)
         return route(
-            number, collective, order, fresh, last, has, coef, gathered(number),
-            row_table, col_table,
+            number, collective, order, fresh, last, has, coef, send, row_taps_f, col_taps_f,
         )
 
     return lax.cond(overflow, lambda: run(4, 1), lambda: run(3, 0))

time: 317 us -> 236 us (0.74)
  Pallas kernels: 255 us -> 216 us
  blocking collectives: 35.7 us -> 0 us
  matrix products: 7.55 us -> 0 us
    pallas_call x1, Pallas kernels: 241 us -> 198 us  [route(): pl.pallas_call(functools.partial(route_kernel, slots, visits, bases), out...]
    all_gather x1 -> x0, blocking collectives: 35.7 us -> none  [local(): lax.all_gather(tags.astype(jnp.int32), ('celly', 'cellx'), axis=0, tiled=...]
    dot_general x2 -> x0, matrix products: 7.55 us -> none  [toeplitz_tables(): jnp.einsum('ijp,bp->bij', picker, taps.astype(jnp.float32))]
    unnamed x8, local copies, waits for them, and re-layouts: 2.15 us -> 6.5 us
    pallas_call x1, Pallas kernels: 14.4 us -> 18.3 us  [local(): pl.pallas_call(gather_kernel, out_shape=[jax.ShapeDtypeStruct((2, slots,...]
    another operation x3 -> x2, local copies, waits for them, and re-layouts: 4.36 us -> 0.91 us
where the time goes in v2:
time: 236 us; the launch traced here: 232 us
  Pallas kernels  216 us (92%)
  local copies, waits for them, and re-layouts  7.88 us (3%)
  other arithmetic  6.7 us (3%)
    pallas_call x1, Pallas kernels, route(): pl.pallas_call(functools.partial(route_kernel, slots, visits, bases), out...  198 us
    pallas_call x1, Pallas kernels, local(): pl.pallas_call(gather_kernel, out_shape=[jax.ShapeDtypeStruct((2, slots,...  18.3 us
    unnamed x8, local copies, waits for them, and re-layouts  6.5 us

profile of v2, /device:TPU:29, one launch (start us, length us, event | category | flops | bytes accessed | tf_op | source)
XLA Modules:
  0.0 232.3 jit_solution(1264164289917917318)
XLA Ops:
  0.7 0.7 fusion.9
  1.3 0.7 and_select_fusion.3
  2.0 0.2 convert_reduce_fusion.6
  2.2 0.2 select_reduce_fusion.2
  2.4 0.7 convert_element_type.44
  3.1 0.7 convert_element_type.45
  3.8 0.7 copy.17
  4.5 0.0 copy-start
  4.5 2.2 copy-done
  6.7 0.0 copy-start.1
  6.7 2.2 copy-done.1
  8.9 18.3 %shard_map.95 = (bf16[2,4,64,128,128]{4,3,2,1,0:T(8,128)(2,1)}, s32[4,4,4,2,8,128]{5,4,3,2,1,0:T(8,128)S(1)}) custom-call(s32[256]{0:T(256)S(1)} %get-tuple-element.87.index_ref, bf16[128,128,128]{2,1,0:T(8,128)(2,1)S(1)} %copy-done, bf16[128,128,128]{2,1,0:T(8,128)(2,1)S(1)} %copy-done.1, s32[8,128]{1,0:T(8,128)S(1)} %scatter.4.tag_ref), custom_call_target="tpu_custom_call" | custom-call | tf_op jit(solution)/shard_map/pallas_call | solution.py:526
  27.3 0.7 fusion.5
  28.6 0.2 reshape_reshape.3
  28.9 0.2 constant_dynamic-slice_fusion
  29.1 0.1 copy.16
  29.2 201.7 %conditional.1 = (f32[256,256]{1,0:T(8,128)S(1)}, f32[256,256]{1,0:T(8,128)S(1)}) conditional(s32[]{:T(128)} %convert_element_type.43, (s32[64,2,4]{0,2,1:T(4,128)S(1)}, s32[]{:T(128)}, f32[20,21]{0,1:T(8,128)S(1)}, f32[7,41]{1,0:T(8,128)S(1)}, f32[7,41]{1,0:T(8,128)S(1)}, /*index=5*/bf16[2,4,4,4,4,128,128]{6,5,4,3,2,1,0:T(8,128)(2,1)}) %tuple.37, ...), branch_computations={%region_4.10_spmd, %region_10.16_spmd} | conditional | flops 1489905 | bytes 31200 | solution.py:588
  29.2 0.1 sub.58
  29.3 0.1 convert_reduce_fusion.1
  29.4 0.6 add_maximum_fusion.last_ref
  30.0 0.6 broadcast_compare_fusion
  30.6 0.1 fusion.1
  30.7 0.6 convert_element_type.32.fresh_ref
  31.3 0.2 convert_reduce_fusion
  31.5 0.7 select_reduce_fusion.order_ref
  32.2 0.7 copy.18.coef_ref
  32.9 197.8 %branch_0_fun.1 = (f32[256,256]{1,0:T(8,128)S(1)}, f32[256,256]{1,0:T(8,128)S(1)}, bf16[2,3,4,4,4,128,128]{6,5,4,3,2,1,0:T(8,128)(2,1)}, bf16[2,3,4,4,4,128,128]{6,5,4,3,2,1,0:T(8,128)(2,1)}) custom-call(s32[256]{0:T(256)} %select_reduce_fusion.order_ref, s32[256]{0:T(256)} %convert_element_type.32.fresh_ref, s32[80]{0:T(128)} %add_maximum_fusion.last_ref, ...), custom_call_target="tpu_custom_call" | custom-call | tf_op jit(solution)/shard_map/cond/branch_0_fun/pallas_call | solution.py:476
  230.9 0.7 copy.29
  231.6 0.7 copy.30
  (9 shorter events, 0.1 us)
Async XLA Ops:
  4.5 2.2 copy-start
  6.7 2.2 copy-start.1

commit v3 on v2

--- a/solution.py
+++ b/solution.py
@@ -11,6 +11,7 @@
 SIDE = 4
 CHIPS = SIDE**3
 EDGE = 32
+STEP = 4
 GROUP = 4
 
 
@@ -29,10 +30,11 @@
     return r
 
 
-def gather_kernel(index_ref, flux_ref, ivar_ref, tag_ref, out_ref, all_ref, send, recv, own):
-    arr, step = pl.program_id(0), pl.program_id(1)
-    per = out_ref.shape[0]
-    now = arr * pl.num_programs(1) + step
+def gather_kernel(
+    index_ref, flux_ref, ivar_ref, tag_ref, flux_out, ivar_out, all_ref, send, recv, own
+):
+    step = pl.program_id(0)
+    per = flux_out.shape[0]
     x, y, z, core = q = coordinates()
     partner = shifted(q, 3, 1, 2)
     whole = slice(None)
@@ -85,20 +87,18 @@
                 for copy in copies(earlier):
                     copy.wait_send()
 
-    pl.when(now == 0)(begin)
-
-    def pick(ref):
-        def body(i, carry):
-            for k in range(4):
-                out_ref[4 * i + k] = ref[index_ref[step * per + 4 * i + k]]
-            return carry
-
-        lax.fori_loop(0, per // 4, body, 0)
-
-    pl.when(arr == 0)(lambda: pick(flux_ref))
-    pl.when(arr == 1)(lambda: pick(ivar_ref))
-    for hop, moment in enumerate((2, 6, 10, 15)):
-        pl.when(now == moment)(functools.partial(advance, hop))
+    pl.when(step == 0)(begin)
+
+    def body(i, carry):
+        for k in range(STEP):
+            block = index_ref[step * per + STEP * i + k]
+            flux_out[STEP * i + k] = flux_ref[block]
+            ivar_out[STEP * i + k] = ivar_ref[block]
+        return carry
+
+    lax.fori_loop(0, per // STEP, body, 0)
+    for hop, moment in enumerate((4, 8, 12, 15)):
+        pl.when(step == moment)(functools.partial(advance, hop))
 
 
 def units_of(slots):
@@ -110,12 +110,12 @@
 
 def route_kernel(
     slots, visits, bases,
-    order_ref, fresh_ref, last_ref, has_ref, coef_ref, rtaps_ref, ctaps_ref, t0,
+    order_ref, fresh_ref, last_ref, has_ref, coef_ref, rtaps_ref, ctaps_ref, t0_flux, t0_ivar,
     numer_out, total_out, t1, t2,
     t_flux, t_ivar, seg, win, matched, strips, got, row_table, col_table, first_ref,
     s1, r1, s2, r2, s3, r3, s4, r4, ls, hs, hr,
 ):
-    t = (t_flux, t_ivar)
+    t, t0 = (t_flux, t_ivar), (t0_flux, t0_ivar)
     q = coordinates()
     row, col = lax.axis_index("celly"), lax.axis_index("cellx")
     rows_n, cols_n = lax.axis_size("celly"), lax.axis_size("cellx")
@@ -154,7 +154,7 @@
         a, b, c = axes(u)
         to = shifted(q, a, d)
         return remote(
-            at(t0, u, (arr,), {a: to[a]}), at(t1, u, (arr,), {a: q[a]}),
+            at(t0[arr], u, (), {a: to[a]}), at(t1, u, (arr,), {a: q[a]}),
             s1.at[arr, u, d], r1.at[arr, u, q[a]], device(to),
         )
 
@@ -164,12 +164,15 @@
         place = at(t1, u, (arr,), {a: asrc})
         return remote(place, place, s1.at[arr, u, da], r1.at[arr, u, asrc], device(q))
 
+    def hopped(arr, u, da, where):
+        return at(t1, u, (arr,), where) if da else at(t0[arr], u, (), where)
+
     def second_hop(arr, u, da, d):
         a, b, c = axes(u)
         to = shifted(q, b, d)
         asrc = lax.rem(q[a] + da, SIDE)
         return remote(
-            at(t0 if da == 0 else t1, u, (arr,), {a: asrc, b: to[b]}),
+            hopped(arr, u, da, {a: asrc, b: to[b]}),
             at(t2, u, (arr,), {a: asrc, b: q[b]}),
             s2.at[arr, u, d, da], r2.at[arr, u, q[b], asrc], device(to),
         )
@@ -189,7 +192,7 @@
         pairs = []
         for da in range(SIDE):
             asrc = lax.rem(q[a] + da, SIDE)
-            source = at(t0 if da == 0 else t1, u, (arr,), {a: asrc, b: bsrc, c: cc})
+            source = hopped(arr, u, da, {a: asrc, b: bsrc, c: cc})
             pairs.append((source, {a: asrc, b: bsrc, c: q[c]}))
         return pairs
 
@@ -234,8 +237,8 @@
             for u in range(count):
                 first_hop(arr, u, d).start()
 
-    def stage2(arr):
-        for da in (0, 1, 3, 2):
+    def stage2(arr, groups=(0, 1, 3, 2)):
+        for da in groups:
             for u in range(count):
                 if da:
                     first_arrival(arr, u, da).wait_recv()
@@ -276,15 +279,17 @@
                     third_whole(arr, u, e, d).wait_send()
 
     def segments(arr):
-        def body(p, total):
-            i = order_ref[p]
-            block = t[arr][i // (CHIPS * slots), (i // CHIPS) % slots,
-                      (i // 16) % 4, (i // 4) % 4, i % 4].astype(jnp.float32)
-            total = jnp.where(fresh_ref[p] > 0, block, total + block)
-            seg[p] = total.astype(jnp.bfloat16)
+        def body(step, total):
+            for k in range(STEP):
+                p = step * STEP + k
+                i = order_ref[p]
+                block = t[arr][i // (CHIPS * slots), (i // CHIPS) % slots,
+                          (i // 16) % 4, (i // 4) % 4, i % 4].astype(jnp.float32)
+                total = jnp.where(fresh_ref[p] > 0, block, total + block)
+                seg[p] = total.astype(jnp.bfloat16)
             return total
 
-        lax.fori_loop(0, seg.shape[0], body, jnp.zeros((128, 128), jnp.float32))
+        lax.fori_loop(0, seg.shape[0] // STEP, body, jnp.zeros((128, 128), jnp.float32))
 
     def summed(key):
         block = seg[last_ref[key]]
@@ -435,10 +440,9 @@
     stage1(0)
     build_tables()
     stage2(0)
+    stage3(0)
     stage1(1)
-    stage3(0)
-    stage2(1)
-    stage3(1, (0,))
+    stage2(1, (0,))
     stage4(0)
     segments(0)
     place_flux()
@@ -449,14 +453,14 @@
     pack_columns()
     to_right.start()
     to_left.start()
-    stage3(1, (1,))
+    stage2(1, (1, 3, 2))
+    stage3(1, (0,))
     to_right.wait()
     to_left.wait()
     unpack_columns()
-    stage3(1, (3,))
-    correlate(0, 2)
-    stage3(1, (2,))
-    correlate(2, visits)
+    correlate(0, visits // 2)
+    stage3(1, (1, 3, 2))
+    correlate(visits // 2, visits)
     stage4(1)
     segments(1)
     combine()
@@ -476,7 +480,7 @@
     coadd, weight, _, _ = pl.pallas_call(
         functools.partial(route_kernel, slots, visits, bases),
         out_shape=[image, image, hop, hop],
-        in_specs=[smem] * 7 + [anywhere],
+        in_specs=[smem] * 7 + [anywhere] * 2,
         out_specs=[vmem] * 2 + [anywhere] * 2,
         scratch_shapes=[
             pltpu.VMEM((2, slots, 4, 4, 4, 128, 128), jnp.bfloat16),
@@ -498,7 +502,7 @@
         compiler_params=pltpu.CompilerParams(
             collective_id=collective, has_side_effects=True, vmem_limit_bytes=63 * 2**20
         ),
-    )(order, fresh, last, has, coef, row_taps, col_taps, send)
+    )(order, fresh, last, has, coef, row_taps, col_taps, *send)
     return coadd, weight
 
 
@@ -522,25 +526,20 @@
     tags = jnp.zeros((8, 128), jnp.int32).at[: slots * CHIPS // 128].set(
         tags.astype(jnp.int32).reshape(-1, 128)
     )
-    per = 32
-    send, tags = pl.pallas_call(
+    per = slots * CHIPS // 16
+    slot_spec = pl.BlockSpec(
+        (None, per, 128, 128), lambda s, ix: (s // (CHIPS // per), s % (CHIPS // per), 0, 0)
+    )
+    slot_shape = jax.ShapeDtypeStruct((slots, CHIPS, 128, 128), jnp.bfloat16)
+    send_flux, send_ivar, tags = pl.pallas_call(
         gather_kernel,
-        out_shape=[
-            jax.ShapeDtypeStruct((2, slots, CHIPS, 128, 128), jnp.bfloat16),
-            jax.ShapeDtypeStruct((4, 4, 4, 2, 8, 128), jnp.int32),
-        ],
+        out_shape=[slot_shape, slot_shape, jax.ShapeDtypeStruct((4, 4, 4, 2, 8, 128), jnp.int32)],
         grid_spec=pltpu.PrefetchScalarGridSpec(
             num_scalar_prefetch=1,
-            grid=(2, slots * CHIPS // per),
-            in_specs=[pl.BlockSpec((blocks, 128, 128), lambda a, s, ix: (0, 0, 0))] * 2
+            grid=(16,),
+            in_specs=[pl.BlockSpec((blocks, 128, 128), lambda s, ix: (0, 0, 0))] * 2
             + [pl.BlockSpec(memory_space=pltpu.VMEM)],
-            out_specs=[
-                pl.BlockSpec(
-                    (None, None, per, 128, 128),
-                    lambda a, s, ix: (a, s // (CHIPS // per), s % (CHIPS // per), 0, 0),
-                ),
-                pl.BlockSpec(memory_space=pl.ANY),
-            ],
+            out_specs=[slot_spec, slot_spec, pl.BlockSpec(memory_space=pl.ANY)],
             scratch_shapes=[
                 pltpu.SemaphoreType.DMA((4, 4)),
                 pltpu.SemaphoreType.DMA((4, 4)),
@@ -551,7 +550,7 @@
             collective_id=2, has_side_effects=True, vmem_limit_bytes=40 * 2**20
         ),
     )(index, flux_blocks, ivar_blocks, tags)
-    send = send.reshape(2, slots, 4, 4, 4, 128, 128)
+    send = [part.reshape(slots, 4, 4, 4, 128, 128) for part in (send_flux, send_ivar)]
     tags = tags[:, :, :, :, : slots * CHIPS // 128].reshape(2 * CHIPS, slots * CHIPS)
 
     mine = lax.dynamic_index_in_dim(

time: 236 us -> 272 us (1.15)
  Pallas kernels: 216 us -> 251 us
    pallas_call x1, Pallas kernels: 198 us -> 232 us  [route(): pl.pallas_call(functools.partial(route_kernel, slots, visits, bases), out...]
where the time goes in v3:
time: 272 us; the launch traced here: 268 us
  Pallas kernels  251 us (92%)
  local copies, waits for them, and re-layouts  7.88 us (3%)
  other arithmetic  6.71 us (2%)
    pallas_call x1, Pallas kernels, route(): pl.pallas_call(functools.partial(route_kernel, slots, visits, bases), out...  232 us
    pallas_call x1, Pallas kernels, local(): pl.pallas_call(gather_kernel, out_shape=[slot_shape, slot_shape, jax.Shap...  18.9 us
    unnamed x8, local copies, waits for them, and re-layouts  6.5 us

profile of v3, /device:TPU:29, one launch (start us, length us, event | category | flops | bytes accessed | tf_op | source)
XLA Modules:
  0.0 267.5 jit_solution(13202103361097602500)
XLA Ops:
  0.7 0.7 fusion.9
  1.3 0.7 and_select_fusion.3
  2.0 0.2 convert_reduce_fusion.6
  2.2 0.2 select_reduce_fusion.2
  2.4 0.7 convert_element_type.44
  3.1 0.7 convert_element_type.45
  3.8 0.7 copy.17
  4.5 0.0 copy-start
  4.5 2.2 copy-done
  6.7 0.0 copy-start.1
  6.7 2.2 copy-done.1
  8.9 18.9 %shard_map.95 = (bf16[4,64,128,128]{3,2,1,0:T(8,128)(2,1)}, bf16[4,64,128,128]{3,2,1,0:T(8,128)(2,1)}, s32[4,4,4,2,8,128]{5,4,3,2,1,0:T(8,128)S(1)}) custom-call(s32[256]{0:T(256)S(1)} %get-tuple-element.99.index_ref, bf16[128,128,128]{2,1,0:T(8,128)(2,1)S(1)} %copy-done, bf16[128,128,128]{2,1,0:T(8,128)(2,1)S(1)} %copy-done.1, s32[8,128]{1,0:T(8,128)S(1)} %scatter.4.tag_ref), custom_call_target="tpu_custom_call" | custom-call | tf_op jit(solution)/shard_map/pallas_call | solution.py:534
  27.8 0.7 fusion.5
  29.2 0.2 reshape_reshape.3
  29.4 0.2 constant_dynamic-slice_fusion
  29.6 0.1 copy.16
  29.7 236.3 %conditional.1 = (f32[256,256]{1,0:T(8,128)S(1)}, f32[256,256]{1,0:T(8,128)S(1)}) conditional(s32[]{:T(128)} %convert_element_type.43, (s32[64,2,4]{0,2,1:T(4,128)S(1)}, s32[]{:T(128)}, f32[20,21]{0,1:T(8,128)S(1)}, f32[7,41]{1,0:T(8,128)S(1)}, f32[7,41]{1,0:T(8,128)S(1)}, /*index=5*/bf16[4,4,4,4,128,128]{5,4,3,2,1,0:T(8,128)(2,1)}, ...), branch_computations={%region_4.10_spmd, %region_10.16_spmd} | conditional | flops 1489905 | bytes 31200 | solution.py:587
  30.0 0.1 sub.63
  30.1 0.1 convert_reduce_fusion.4
  30.2 0.5 add_maximum_fusion.1.last_ref
  30.7 0.6 broadcast_compare_fusion.1
  31.3 0.1 fusion.3
  31.4 0.6 convert_element_type.37.fresh_ref
  32.0 0.2 convert_reduce_fusion.3
  32.2 0.7 select_reduce_fusion.1.order_ref
  33.0 0.7 copy.19.coef_ref
  33.6 232.4 %branch_1_fun.1 = (f32[256,256]{1,0:T(8,128)S(1)}, f32[256,256]{1,0:T(8,128)S(1)}, bf16[2,4,4,4,4,128,128]{6,5,4,3,2,1,0:T(8,128)(2,1)}, bf16[2,4,4,4,4,128,128]{6,5,4,3,2,1,0:T(8,128)(2,1)}) custom-call(s32[256]{0:T(256)} %select_reduce_fusion.1.order_ref, s32[256]{0:T(256)} %convert_element_type.37.fresh_ref, s32[80]{0:T(128)} %add_maximum_fusion.1.last_ref, ...), custom_call_target="tpu_custom_call" | custom-call | tf_op jit(solution)/shard_map/cond/branch_1_fun/pallas_call | solution.py:480
  266.1 0.7 copy.29
  266.8 0.7 copy.30
  (9 shorter events, 0.1 us)
Async XLA Ops:
  4.5 2.2 copy-start
  6.7 2.2 copy-start.1
